TPU v7x, 32 devices: a whole 2x2x4 slice. The times are simulated.
32 devices in a mesh: rows: 16 (over z, y, core), cols: 2 (over x).
Axes of the slice: x: 2, y: 2, z: 4, core: 2. Of those that a mesh axis runs over, the one named last changes fastest.
Arguments:
- elevation: float32 [512, 1024], P('rows', 'cols'), may hold values from -4.5 to 4.5
- water_depth: float32 [512, 1024], P('rows', 'cols'), may hold values from 1 to 40
- friction: float32 [512, 1024], P('rows', 'cols'), may hold values from 0.1 to 2
- current_x: float32 [512, 1024], P('rows', 'cols'), may hold values from -0.9 to 0.9
- wet_mask: int32 [512, 1024], P('rows', 'cols'), may hold values from 0 to 1, as said below
Outputs:
- new_elevation: float32 [512, 1024], P('rows', 'cols')
Inputs may be any that keep to these rules, and one draw needn't show every extreme that they name: `wet_mask`: 1 marks a wet cell, 0 a dry one.
All inputs are finite; a program needn't handle non-finite values.
Results may differ from a plain program's by a relative error of at most 0.0003.
Values sent between devices are 32-bit elements; how exact they have to be, the bound alone decides.
A program may use at most 64 MiB of HBM per device.

v0:
```python
import jax
import jax.numpy as jnp
from jax import lax
from jax.sharding import PartitionSpec as P

coupling = 100.0


def padded_2(shard, sides, width):
    for axis, dim in sides:
        count, length = (lax.axis_size(axis), shard.shape[dim])
        up = [(i, (i + 1) % count) for i in range(count - 1)]
        down = [(j, i) for i, j in up]
        last = lax.slice_in_dim(shard, length - width, length, axis=dim)
        first = lax.slice_in_dim(shard, 0, width, axis=dim)
        before = lax.ppermute(last, axis, up)
        after = lax.ppermute(first, axis, down)
        shard = jnp.concatenate([before, shard, after], axis=dim)
    return shard


def face_weights(wet_depth):
    interior = coupling * jnp.sqrt(wet_depth[:, :-1] * wet_depth[:, 1:])
    return jnp.concatenate([interior, jnp.zeros_like(wet_depth[:, :1])], axis=1)


def advect_padded(padded, values, courant):
    forward = padded[:, 2:]
    backward = padded[:, :-2]
    return 0.5 * courant * (forward - backward) - 0.5 * courant * courant * (
        forward - 2.0 * values + backward
    )


def neighbour(values, stride, filler, forward):
    padding = jnp.full(values.shape[:-1] + (stride,), filler, values.dtype)
    if forward:
        return jnp.concatenate([values[..., stride:], padding], axis=-1)
    return jnp.concatenate([padding, values[..., :-stride]], axis=-1)


def reduce_system(sub_diag, middle, super_diag, right_side):
    line_length = middle.shape[-1]
    stride = 1
    while stride < line_length:
        weight_low = -sub_diag / neighbour(middle, stride, 1.0, False)
        weight_high = -super_diag / neighbour(middle, stride, 1.0, True)
        next_sub = weight_low * neighbour(sub_diag, stride, 0.0, False)
        next_super = weight_high * neighbour(super_diag, stride, 0.0, True)
        middle = (
            middle
            + weight_low * neighbour(super_diag, stride, 0.0, False)
            + weight_high * neighbour(sub_diag, stride, 0.0, True)
        )
        right_side = (
            right_side
            + weight_low * neighbour(right_side, stride, 0.0, False)
            + weight_high * neighbour(right_side, stride, 0.0, True)
        )
        sub_diag = next_sub
        super_diag = next_super
        stride = stride * 2
    return right_side / middle


def reduce_lines(couplings, damping, right_side):
    left_faces = jnp.concatenate([jnp.zeros_like(couplings[:, :1]), couplings[:, :-1]], axis=1)
    sub_diag = -0.5 * left_faces
    super_diag = -0.5 * couplings
    middle = 1.0 + damping + 0.5 * (left_faces + couplings)
    return reduce_system(sub_diag, middle, super_diag, right_side[None])[0]


def on_device(elevation, water_depth, friction, current_x, wet_mask):
    wet_depth = water_depth * wet_mask.astype(jnp.float32)
    damping = friction / (4.0 * water_depth)
    first_rhs = (1.0 - damping) * elevation
    line_data = lax.all_to_all(
        jnp.stack([first_rhs, wet_depth, damping]), "cols", split_axis=1, concat_axis=2, tiled=True
    )
    half_step = reduce_lines(face_weights(line_data[1]), line_data[2], line_data[0])
    half_block = lax.all_to_all(half_step, "cols", split_axis=1, concat_axis=0, tiled=True)
    padded = padded_2(half_block, (("cols", 1),), 1)
    second_rhs = (1.0 - damping) * half_block - advect_padded(padded, half_block, current_x)
    second_cols = second_rhs.T
    columns = lax.all_to_all(
        jnp.stack([second_cols, wet_depth.T, damping.T]),
        "rows",
        split_axis=1,
        concat_axis=2,
        tiled=True,
    )
    updated = reduce_lines(face_weights(columns[1]), columns[2], columns[0])
    returned = lax.all_to_all(updated, "rows", split_axis=1, concat_axis=0, tiled=True)
    return returned.T


def solution(mesh):
    placed = (
        P("rows", "cols"),
        P("rows", "cols"),
        P("rows", "cols"),
        P("rows", "cols"),
        P("rows", "cols"),
    )
    return jax.shard_map(
        on_device, mesh=mesh, in_specs=placed, out_specs=P("rows", "cols"), check_vma=False
    )
```

profile of v0, /device:TPU:0, one launch (start us, length us, event | category | flops | bytes accessed | tf_op | source)
XLA Modules:
  0.0 65.2 jit_solution(15124438412772697161)
XLA Ops:
  0.0 1.0 %fusion.47 = (f32[1,32,512]{2,1,0:T(8,128)S(1)}, f32[1,512,32]{1,2,0:T(8,128)S(1)}, f32[1,32,512]{2,1,0:T(8,128)S(1)}, f32[32,512]{1,0:T(8,128)S(1)}) fusion(f32[32,512]{1,0:T(8,128)} %param.6, s32[32,512]{1,0:T(8,128)} %param.9, f32[32,512]{1,0:T(8,128)} %param.5, f32[32,512]{1,0:T(8,128)} %param.7), kind=kLoop, calls=%fused_computation.193 | loop fusion | flops 98304 | bytes 524288 | tf_op jit(solution)/shard_map/stack | solution.py:79
  1.0 0.1 copy.21
  1.1 9.2 %all_to_all.68 = f32[3,32,512]{2,0,1:T(4,128)S(1)} all-to-all(f32[3,32,512]{2,0,1:T(4,128)S(1)} %copy.21), channel_id=1, replica_groups=mesh['rows'=16,'cols'=2] {'cols'}, dimensions={1} | all-to-all | bytes 393216 | tf_op jit(solution)/shard_map/all_to_all | solution.py:78
  10.3 0.2 copy.34
  10.5 0.1 fusion.7
  10.7 0.1 pad_multiply_fusion.36
  10.9 0.1 fusion.117
  11.0 0.1 multiply_add_fusion.17
  11.3 0.1 fusion.44
  11.5 0.2 fusion.42
  11.8 0.1 fusion.113
  11.9 0.1 multiply_add_fusion.16
  12.1 0.1 fusion.40
  12.5 0.1 fusion.109
  12.5 0.1 multiply_add_fusion.15
  12.7 0.1 fusion.38
  13.1 0.1 fusion.105
  13.1 0.1 multiply_add_fusion.14
  13.3 0.1 fusion.36
  13.7 0.1 multiply_add_fusion.13
  14.0 0.1 fusion.34
  14.4 0.1 multiply_add_fusion.12
  14.6 0.1 fusion.32
  14.9 0.1 multiply_add_fusion.11
  15.0 0.1 fusion.30
  15.6 6.5 %all_to_all.69 = f32[16,2,512]{2,0,1:T(8,128)S(1)} all-to-all(f32[16,2,512]{2,0,1:T(8,128)S(1)} %copy.23), channel_id=1, replica_groups=mesh['rows'=16,'cols'=2] {'cols'}, dimensions={1} | all-to-all | bytes 131072 | tf_op jit(solution)/shard_map/all_to_all | solution.py:82
  22.2 1.9 %collective-permute-start.1 = (f32[32,1]{1,0:T(8,128)S(1)}, f32[32,1]{1,0:T(8,128)S(1)}, u32[]{:S(2)}, u32[]{:S(2)}) collective-permute-start(f32[32,1]{1,0:T(8,128)S(1)} %get-tuple-element.137), channel_id=1, source_target_pairs={{0,1},{2,3},{4,5},{6,7},{8,9},{10,11},{12,13},{14,15},{16,17},{18,... | collective-permute-start | bytes 392 | tf_op jit(solution)/shard_map/ppermute | solution.py:16
  24.1 1.3 %collective-permute-start = (f32[32,1]{1,0:T(8,128)S(1)}, f32[32,1]{1,0:T(8,128)S(1)}, u32[]{:S(2)}, u32[]{:S(2)}) collective-permute-start(f32[32,1]{1,0:T(8,128)S(1)} %get-tuple-element.138), channel_id=1, source_target_pairs={{1,0},{3,2},{5,4},{7,6},{9,8},{11,10},{13,12},{15,14},{17,16},{19,... | collective-permute-start | bytes 392 | tf_op jit(solution)/shard_map/ppermute | solution.py:17
  25.4 0.1 collective-permute-done.1
  25.5 4.2 %collective-permute-done = f32[32,1]{1,0:T(8,128)S(1)} collective-permute-done((f32[32,1]{1,0:T(8,128)S(1)}, f32[32,1]{1,0:T(8,128)S(1)}, u32[]{:S(2)}, u32[]{:S(2)}) %collective-permute-start) | collective-permute-done | bytes 160 | tf_op jit(solution)/shard_map/ppermute | solution.py:17
  29.7 0.1 fusion.2
  29.8 0.4 copy.24
  30.2 0.6 reshape.22
  30.9 14.8 %all_to_all.70 = f32[16,1,3072]{2,1,0:T(1,128)S(1)} all-to-all(f32[16,1,3072]{2,1,0:T(1,128)S(1)} %reshape.22), channel_id=1, replica_groups=mesh['rows'=16,'cols'=2] {'rows'}, dimensions={0} | all-to-all | bytes 393216 | tf_op jit(solution)/shard_map/all_to_all | solution.py:86
  45.7 0.5 broadcast.429
  46.2 1.1 %reduce = f32[16,3072]{1,0:T(8,128)S(1)} reduce(f32[16,1,3072]{2,1,0:T(1,128)S(1)} %all_to_all.70, f32[]{:T(128)} %broadcast.429), dimensions={1}, to_apply=%all_to_all.57.reduce_sub_computation | reduce | bytes 393220 | tf_op jit(solution)/shard_map/all_to_all | solution.py:86
  47.3 0.6 reshape.23
  48.0 0.5 copy.33
  48.5 0.1 squeeze.5
  48.7 0.1 fusion.5
  48.8 0.1 slice.587
  48.9 0.1 add.609
  49.4 0.1 multiply_add_fusion.7
  49.7 0.1 fusion.24
  49.9 0.2 fusion.22
  50.3 0.1 multiply_add_fusion.6
  50.5 0.1 fusion.20
  50.9 0.1 multiply_add_fusion.5
  51.1 0.1 fusion.18
  51.5 0.1 multiply_add_fusion.4
  51.7 0.1 fusion.16
  52.1 0.1 multiply_add_fusion.3
  52.3 0.1 fusion.14
  52.7 0.1 multiply_add_fusion.2
  52.9 0.1 fusion.12
  53.3 0.1 multiply_add_fusion.1
  53.4 0.1 fusion.10
  53.7 0.1 all_to_all.60
  53.8 0.1 copy.35
  53.9 0.2 reshape.24
  54.1 9.5 %all_to_all.71 = f32[16,1,1024]{2,1,0:T(1,128)S(1)} all-to-all(f32[16,1,1024]{2,1,0:T(1,128)S(1)} %reshape.24), channel_id=1, replica_groups=mesh['rows'=16,'cols'=2] {'rows'}, dimensions={0} | all-to-all | bytes 131072 | tf_op jit(solution)/shard_map/all_to_all | solution.py:94
  63.6 0.8 %reduce.1 = f32[16,1024]{1,0:T(8,128)S(1)} reduce(f32[16,1,1024]{2,1,0:T(1,128)S(1)} %all_to_all.71, f32[]{:T(128)} %broadcast.429), dimensions={1}, to_apply=%all_to_all.61.reduce_sub_computation | reduce | bytes 131076 | tf_op jit(solution)/shard_map/all_to_all | solution.py:94
  64.4 0.1 reshape.25
  64.5 0.7 %copy.27 = f32[512,32]{0,1:T(8,128)} copy(f32[512,32]{1,0:T(8,128)S(1)} %bitcast.250) | data formatting | bytes 131072 | tf_op jit(solution)/shard_map/all_to_all | solution.py:94
  (90 shorter events, 5.0 us)
Async XLA Ops:
  22.1 7.6 %copy-start = (f32[32,512]{1,0:T(8,128)S(1)}, f32[32,512]{1,0:T(8,128)}, u32[]{:S(2)}) copy-start(f32[32,512]{1,0:T(8,128)} %param.8) | copy-start | bytes 196612
  22.2 3.3 %collective-permute-start.1 = (f32[32,1]{1,0:T(8,128)S(1)}, f32[32,1]{1,0:T(8,128)S(1)}, u32[]{:S(2)}, u32[]{:S(2)}) collective-permute-start(f32[32,1]{1,0:T(8,128)S(1)} %get-tuple-element.137), channel_id=1, source_target_pairs={{0,1},{2,3},{4,5},{6,7},{8,9},{10,11},{12,13},{14,15},{16,17},{18,... | collective-permute-start | bytes 392 | tf_op jit(solution)/shard_map/ppermute | solution.py:16
  24.1 5.6 %collective-permute-start = (f32[32,1]{1,0:T(8,128)S(1)}, f32[32,1]{1,0:T(8,128)S(1)}, u32[]{:S(2)}, u32[]{:S(2)}) collective-permute-start(f32[32,1]{1,0:T(8,128)S(1)} %get-tuple-element.138), channel_id=1, source_target_pairs={{1,0},{3,2},{5,4},{7,6},{9,8},{11,10},{13,12},{15,14},{17,16},{19,... | collective-permute-start | bytes 392 | tf_op jit(solution)/shard_map/ppermute | solution.py:17
where the time goes:
time: 65.6 us; the launch traced here: 65.2 us
  blocking collectives  40 us (61%)
  local copies, waits for them, and re-layouts  9.44 us (14%)
  other arithmetic  7.63 us (12%)
  waiting for transfers between devices  4.33 us (7%)
  starting transfers between devices  3.2 us (5%)
    all_to_all x1, blocking collectives, on_device(): lax.all_to_all(jnp.stack([second_cols, wet_depth.T, damping.T]), 'rows',...  14.8 us
    all_to_all x1, blocking collectives, on_device(): lax.all_to_all(updated, 'rows', split_axis=1, concat_axis=0, tiled=True)  9.48 us
    all_to_all x1, blocking collectives, on_device(): lax.all_to_all(jnp.stack([first_rhs, wet_depth, damping]), 'cols', split_...  9.18 us
    all_to_all x1, blocking collectives, on_device(): lax.all_to_all(half_step, 'cols', split_axis=1, concat_axis=0, tiled=True)  6.5 us
    ppermute x1, waiting for transfers between devices, padded_2(): after = lax.ppermute(first, axis, down)  4.21 us
    slice x38, local copies, waits for them, and re-layouts, neighbour(): return jnp.concatenate([padding, values[..., :-stride]], axis=-1)  2.4 us
    add x17, other arithmetic, reduce_system(): right_side + weight_low * neighbour(right_side, stride, 0.0, False)  2.33 us
    slice x37, local copies, waits for them, and re-layouts, neighbour(): return jnp.concatenate([values[..., stride:], padding], axis=-1)  2.26 us
  transfers between devices with their start and end apart: 2, of which 2 were waited for; matrix products, arithmetic and copies ran while one was open for 0% of the time, Pallas kernels for 0%

commit v1 on v0

v1 whole, which is shorter than its diff:
```python
import functools

import jax
import jax.numpy as jnp
from jax import lax
from jax.experimental import pallas as pl
from jax.experimental.pallas import tpu as pltpu
from jax.sharding import PartitionSpec as P

half_coupling = 50.0
LANES = 128


def rolled(values, shift, axis):
    return pltpu.roll(values, shift % values.shape[axis], axis)


def reduce_lines(face, excess, rights, axis):
    length = face.shape[axis]
    before = rolled(face, 1, axis)
    stride = 1
    while stride < length:
        inverse = 1.0 / (excess + before + face)
        to_next = face * inverse
        to_prev = before * inverse
        through = to_next * before
        excess = (
            excess
            + rolled(to_next * excess, stride, axis)
            + rolled(to_prev * excess, -stride, axis)
        )
        rights = [
            right
            + rolled(to_next * right, stride, axis)
            + rolled(to_prev * right, -stride, axis)
            for right in rights
        ]
        face = rolled(through, -stride, axis)
        before = rolled(through, stride, axis)
        stride *= 2
    inverse = 1.0 / excess
    return [right * inverse for right in rights]


def reduce_fluxes(lower, middle, upper, rights):
    count = len(middle)
    stride = 1
    while stride < count:
        inverse = [1.0 / m for m in middle]
        new_lower, new_middle, new_upper = [], [], []
        new_rights = [[] for _ in rights]
        for k in range(count):
            a, c, m = None, None, middle[k]
            sums = [right[k] for right in rights]
            if k - stride >= 0:
                w = lower[k] * inverse[k - stride]
                if k - 2 * stride >= 0:
                    a = w * lower[k - stride]
                m = m - w * upper[k - stride]
                sums = [s + w * right[k - stride] for s, right in zip(sums, rights)]
            if k + stride < count:
                w = upper[k] * inverse[k + stride]
                if k + 2 * stride < count:
                    c = w * upper[k + stride]
                m = m - w * lower[k + stride]
                sums = [s + w * right[k + stride] for s, right in zip(sums, rights)]
            new_lower.append(a)
            new_middle.append(m)
            new_upper.append(c)
            for out, s in zip(new_rights, sums):
                out.append(s)
        lower, middle, upper, rights = new_lower, new_middle, new_upper, new_rights
        stride *= 2
    inverse = [1.0 / m for m in middle]
    return [[s * i for s, i in zip(right, inverse)] for right in rights]


def flux_system(weights, first_first, last_first, last_last):
    count = len(weights)
    lower = [weights[k] * last_first[k] for k in range(count)]
    upper = [weights[k] * last_first[k + 1] for k in range(count)]
    middle = [1.0 + weights[k] * (last_last[k] + first_first[k + 1]) for k in range(count)]
    return lower, middle, upper


def step_kernel(
    nr, nc, elevation, depth, friction, current, mask, out,
    xbuf, kbuf, pbuf, x_send, x_recv, k_send, k_recv, p_send, p_recv,
):
    row_at, col_at = lax.axis_index("rows"), lax.axis_index("cols")
    height, width = out.shape
    chunks = width // LANES

    def row_peer(offset):
        return (lax.rem(row_at + offset, nr), col_at)

    def col_peer(offset):
        return (row_at, lax.rem(col_at + offset, nc))

    def row_copies(buffer, send, recv):
        return [
            pltpu.make_async_remote_copy(
                src_ref=buffer.at[row_at], dst_ref=buffer.at[row_at],
                send_sem=send.at[k - 1], recv_sem=recv.at[k - 1],
                device_id=row_peer(k), device_id_type=pl.DeviceIdType.MESH,
            )
            for k in range(1, nr)
        ]

    barrier = pltpu.get_barrier_semaphore()
    for k in range(1, nr):
        pl.semaphore_signal(barrier, inc=1, device_id=row_peer(k), device_id_type=pl.DeviceIdType.MESH)
    for k in range(1, nc):
        pl.semaphore_signal(barrier, inc=1, device_id=col_peer(k), device_id_type=pl.DeviceIdType.MESH)

    still = depth[...]
    wet = still * mask[...].astype(jnp.float32)
    damping = friction[...] / (4.0 * still)
    excess = 1.0 + damping
    lane = lax.broadcasted_iota(jnp.int32, (height, width), 1)
    row = lax.broadcasted_iota(jnp.int32, (height, width), 0)

    face = half_coupling * jnp.sqrt(wet * rolled(wet, -1, 0))
    face = jnp.where(row == height - 1, 0.0, face)
    unit_first = jnp.where(row == 0, 1.0, 0.0)
    unit_last = jnp.where(row == height - 1, 1.0, 0.0)
    from_first, from_last = reduce_lines(face, excess, [unit_first, unit_last], 0)
    ends = (
        from_first[0:1], from_first[height - 1 : height], from_last[height - 1 : height],
        wet[0:1], wet[height - 1 : height],
    )
    for q, line in enumerate(ends):
        for c in range(chunks):
            kbuf[row_at, q, c : c + 1, :] = line[:, c * LANES : (c + 1) * LANES]

    pl.semaphore_wait(barrier, nr + nc - 2)
    k_copies = row_copies(kbuf, k_send, k_recv)
    for copy in k_copies:
        copy.start()

    face_x = half_coupling * jnp.sqrt(wet * rolled(wet, -1, 1))
    face_x = jnp.where(lane == width - 1, 0.0, face_x)
    first_rhs = (1.0 - damping) * elevation[...]
    small = lax.broadcasted_iota(jnp.int32, (height, LANES), 1)
    at_left = col_at == 0
    if nc == 2:
        edge = jnp.where(at_left, width - 1, 0)
        unit = jnp.where(lane == edge, 1.0, 0.0)
        solved, spike = reduce_lines(face_x, excess, [first_rhs, unit], 1)
        message = None
        for q, values in enumerate((solved, spike, wet)):
            chunk = jnp.where(at_left, values[:, width - LANES :], values[:, :LANES])
            chunk = pltpu.roll(chunk, q + jnp.where(at_left, 1, 0), 1)
            message = chunk if q == 0 else jnp.where(small == q, chunk, message)
    else:
        units = [jnp.where(lane == 0, 1.0, 0.0), jnp.where(lane == width - 1, 1.0, 0.0)]
        solved, from_left, from_right = reduce_lines(face_x, excess, [first_rhs] + units, 1)
        message = jnp.zeros((height, LANES), jnp.float32)
        columns = (
            solved[:, 0:1], solved[:, width - 1 : width], from_left[:, 0:1],
            from_left[:, width - 1 : width], from_right[:, width - 1 : width],
            wet[:, 0:1], wet[:, width - 1 : width],
        )
        for q, column in enumerate(columns):
            message = jnp.where(small == q, column, message)
    xbuf[col_at] = message
    x_copies = [
        pltpu.make_async_remote_copy(
            src_ref=xbuf.at[col_at], dst_ref=xbuf.at[col_at],
            send_sem=x_send.at[k - 1], recv_sem=x_recv.at[k - 1],
            device_id=col_peer(k), device_id_type=pl.DeviceIdType.MESH,
        )
        for k in range(1, nc)
    ]
    for copy in x_copies:
        copy.start()
    for copy in x_copies:
        copy.wait_recv()

    if nc == 2:
        other = xbuf[1 - col_at]
        p, s, w = (message[:, q : q + 1] for q in range(3))
        other_p, other_s, other_w = (other[:, q : q + 1] for q in range(3))
        weight = half_coupling * jnp.sqrt(w * other_w)
        flux = weight * (p - other_p) / (1.0 + weight * (s + other_s))
        half_step = solved - spike * flux
        beyond = other_p + other_s * flux
        right_of = jnp.where(at_left, beyond, 0.0)
        left_of = jnp.where(at_left, 0.0, beyond)
    else:
        got = [xbuf[k] for k in range(nc)]
        pf, pb, ff, fl, ll, wf, wl = ([g[:, q : q + 1] for g in got] for q in range(7))
        weights = [half_coupling * jnp.sqrt(wl[k] * wf[k + 1]) for k in range(nc - 1)]
        system = flux_system(weights, ff, fl, ll)
        (fluxes,) = reduce_fluxes(
            *system, [[weights[k] * (pb[k] - pf[k + 1]) for k in range(nc - 1)]]
        )
        zero = jnp.zeros_like(fluxes[0])
        fluxes = [zero] + fluxes + [zero]
        first = [pf[k] + ff[k] * fluxes[k] - fl[k] * fluxes[k + 1] for k in range(nc)] + [zero]
        last = [zero] + [pb[k] + fl[k] * fluxes[k] - ll[k] * fluxes[k + 1] for k in range(nc)]
        entering, leaving, left_of, right_of = zero, zero, zero, zero
        for k in range(nc):
            here = col_at == k
            entering = jnp.where(here, fluxes[k], entering)
            leaving = jnp.where(here, fluxes[k + 1], leaving)
            left_of = jnp.where(here, last[k], left_of)
            right_of = jnp.where(here, first[k + 1], right_of)
        half_step = solved + from_left * entering - from_right * leaving

    courant = current[...]
    forward = jnp.where(lane == width - 1, right_of, rolled(half_step, -1, 1))
    backward = jnp.where(lane == 0, left_of, rolled(half_step, 1, 1))
    advected = 0.5 * courant * (forward - backward) - 0.5 * courant * courant * (
        forward - 2.0 * half_step + backward
    )
    second_rhs = (1.0 - damping) * half_step - advected

    for q, response in enumerate((from_first, from_last)):
        line = jnp.sum(response * second_rhs, axis=0, keepdims=True)
        for c in range(chunks):
            pbuf[row_at, q, c : c + 1, :] = line[:, c * LANES : (c + 1) * LANES]
    p_copies = row_copies(pbuf, p_send, p_recv)
    for copy in p_copies:
        copy.start()

    (solved_y,) = reduce_lines(face, excess, [second_rhs], 0)

    for copy in k_copies:
        copy.wait_recv()
    ff, fl, ll, wf, wl = ([kbuf[k, q] for k in range(nr)] for q in range(5))
    weights = [half_coupling * jnp.sqrt(wl[k] * wf[k + 1]) for k in range(nr - 1)]
    system = flux_system(weights, ff, fl, ll)
    rights = [
        [jnp.where(row_at + shift == k, weights[k], 0.0) for k in range(nr - 1)]
        for shift in (-1, 0)
    ]
    into, outof = reduce_fluxes(*system, rights)

    for copy in p_copies:
        copy.wait_recv()
    entering = leaving = jnp.zeros((chunks, LANES), jnp.float32)
    for k in range(nr - 1):
        jump = pbuf[k, 1] - pbuf[k + 1, 0]
        entering = entering + into[k] * jump
        leaving = leaving + outof[k] * jump
    for c in range(chunks):
        at = slice(c * LANES, (c + 1) * LANES)
        out[:, at] = (
            solved_y[:, at]
            + from_first[:, at] * entering[c : c + 1, :]
            - from_last[:, at] * leaving[c : c + 1, :]
        )

    for copy in k_copies + x_copies + p_copies:
        copy.wait_send()


def on_device(elevation, water_depth, friction, current_x, wet_mask):
    nr, nc = lax.axis_size("rows"), lax.axis_size("cols")
    height, width = elevation.shape
    chunks = width // LANES
    return pl.pallas_call(
        functools.partial(step_kernel, nr, nc),
        out_shape=jax.ShapeDtypeStruct(elevation.shape, jnp.float32),
        in_specs=[pl.BlockSpec(memory_space=pltpu.VMEM)] * 5,
        out_specs=pl.BlockSpec(memory_space=pltpu.VMEM),
        scratch_shapes=[
            pltpu.VMEM((nc, height, LANES), jnp.float32),
            pltpu.VMEM((nr, 5, chunks, LANES), jnp.float32),
            pltpu.VMEM((nr, 2, chunks, LANES), jnp.float32),
            pltpu.SemaphoreType.DMA((nc - 1,)),
            pltpu.SemaphoreType.DMA((nc - 1,)),
            pltpu.SemaphoreType.DMA((nr - 1,)),
            pltpu.SemaphoreType.DMA((nr - 1,)),
            pltpu.SemaphoreType.DMA((nr - 1,)),
            pltpu.SemaphoreType.DMA((nr - 1,)),
        ],
        compiler_params=pltpu.CompilerParams(
            collective_id=0, has_side_effects=True, vmem_limit_bytes=32 * 1024 * 1024
        ),
    )(elevation, water_depth, friction, current_x, wet_mask)


def solution(mesh):
    placed = P("rows", "cols")
    return jax.shard_map(
        on_device, mesh=mesh, in_specs=(placed,) * 5, out_specs=placed, check_vma=False
    )
```

time: 65.6 us -> 19.6 us (0.30)
  blocking collectives: 40 us -> 0 us
  Pallas kernels: 0 us -> 14.4 us
  other arithmetic: 7.63 us -> 0 us
  local copies, waits for them, and re-layouts: 9.44 us -> 4.83 us
  waiting for transfers between devices: 4.33 us -> 0 us
  starting transfers between devices: 3.2 us -> 0 us
    all_to_all x4 -> x0, blocking collectives: 40 us -> none  [the longest x1 14.8 us: on_device(): lax.all_to_all(jnp.stack([second_cols, wet_depth.T, damping.T]), 'rows',...]
    pallas_call x0 -> x1, Pallas kernels: none -> 14.4 us  [on_device(): pl.pallas_call(functools.partial(step_kernel, nr, nc), out_shape=jax.Shap...]
    slice x78 -> x0, local copies, waits for them, and re-layouts: 4.93 us -> none  [the longest x38 2.4 us: neighbour(): return jnp.concatenate([padding, values[..., :-stride]], axis=-1)]
    ppermute x2 -> x0, waiting for transfers between devices: 4.33 us -> none  [the longest x1 4.21 us: padded_2(): after = lax.ppermute(first, axis, down)]
    add x32 -> x0, other arithmetic: 4 us -> none  [the longest x17 2.33 us: reduce_system(): right_side + weight_low * neighbour(right_side, stride, 0.0, False)]
    unnamed x8 -> x11, local copies, waits for them, and re-layouts: 1.56 us -> 4.83 us
    ppermute x2 -> x0, starting transfers between devices: 3.2 us -> none  [the longest x1 1.91 us: padded_2(): before = lax.ppermute(last, axis, up)]
    all_to_all x8 -> x0, local copies, waits for them, and re-layouts: 2.14 us -> none  [the longest x2 0.97 us: on_device(): lax.all_to_all(jnp.stack([second_cols, wet_depth.T, damping.T]), 'rows',...]
  transfers between devices with their start and end apart: 2 -> 0, of which waited for: 2 -> 0; matrix products, arithmetic and copies ran while one was open for 0% -> 0% of each run, Pallas kernels for 0% -> 0%
where the time goes in v1:
time: 19.6 us; the launch traced here: 19.3 us
  Pallas kernels  14.4 us (73%)
  local copies, waits for them, and re-layouts  4.83 us (25%)
    pallas_call x1, Pallas kernels, on_device(): pl.pallas_call(functools.partial(step_kernel, nr, nc), out_shape=jax.Shap...  14.4 us
    unnamed x11, local copies, waits for them, and re-layouts  4.83 us

profile of v1, /device:TPU:0, one launch (start us, length us, event | category | flops | bytes accessed | tf_op | source)
XLA Modules:
  0.0 19.3 jit_solution(9907369143146102911)
XLA Ops:
  0.0 0.0 copy-start
  0.0 0.8 %copy-done = f32[32,512]{1,0:T(8,128)S(1)} copy-done((f32[32,512]{1,0:T(8,128)S(1)}, f32[32,512]{1,0:T(8,128)}, u32[]{:S(2)}) %copy-start) | copy-done | bytes 65560
  0.8 0.0 copy-start.1
  0.8 0.8 %copy-done.1 = f32[32,512]{1,0:T(8,128)S(1)} copy-done((f32[32,512]{1,0:T(8,128)S(1)}, f32[32,512]{1,0:T(8,128)}, u32[]{:S(2)}) %copy-start.1) | copy-done | bytes 65560
  1.7 0.0 copy-start.2
  1.7 0.8 %copy-done.2 = f32[32,512]{1,0:T(8,128)S(1)} copy-done((f32[32,512]{1,0:T(8,128)S(1)}, f32[32,512]{1,0:T(8,128)}, u32[]{:S(2)}) %copy-start.2) | copy-done | bytes 65560
  2.5 0.0 copy-start.3
  2.5 0.8 %copy-done.3 = f32[32,512]{1,0:T(8,128)S(1)} copy-done((f32[32,512]{1,0:T(8,128)S(1)}, f32[32,512]{1,0:T(8,128)}, u32[]{:S(2)}) %copy-start.3) | copy-done | bytes 65560
  3.4 0.0 copy-start.4
  3.4 0.8 %copy-done.4 = s32[32,512]{1,0:T(8,128)S(1)} copy-done((s32[32,512]{1,0:T(8,128)S(1)}, s32[32,512]{1,0:T(8,128)}, u32[]{:S(2)}) %copy-start.4) | copy-done | bytes 65560
  4.2 14.4 %shard_map.55 = f32[32,512]{1,0:T(8,128)S(1)} custom-call(f32[32,512]{1,0:T(8,128)S(1)} %copy-done, f32[32,512]{1,0:T(8,128)S(1)} %copy-done.1, f32[32,512]{1,0:T(8,128)S(1)} %copy-done.2, f32[32,512]{1,0:T(8,128)S(1)} %copy-done.3, s32[32,512]{1,0:T(8,128)S(1)} %copy-done.4), custom_call_target="tpu_custom_call" | custom-call | tf_op jit(solution)/shard_map/pallas_call | solution.py:263
  18.6 0.6 %copy.7 = f32[32,512]{1,0:T(8,128)} copy(f32[32,512]{1,0:T(8,128)S(1)} %shard_map.55) | data formatting | bytes 131072
Async XLA Ops:
  0.0 0.8 %copy-start = (f32[32,512]{1,0:T(8,128)S(1)}, f32[32,512]{1,0:T(8,128)}, u32[]{:S(2)}) copy-start(f32[32,512]{1,0:T(8,128)} %elevation.1) | copy-start | bytes 196612
  0.8 0.8 %copy-start.1 = (f32[32,512]{1,0:T(8,128)S(1)}, f32[32,512]{1,0:T(8,128)}, u32[]{:S(2)}) copy-start(f32[32,512]{1,0:T(8,128)} %depth.1) | copy-start | bytes 196612
  1.7 0.8 %copy-start.2 = (f32[32,512]{1,0:T(8,128)S(1)}, f32[32,512]{1,0:T(8,128)}, u32[]{:S(2)}) copy-start(f32[32,512]{1,0:T(8,128)} %friction.1) | copy-start | bytes 196612
  2.5 0.8 %copy-start.3 = (f32[32,512]{1,0:T(8,128)S(1)}, f32[32,512]{1,0:T(8,128)}, u32[]{:S(2)}) copy-start(f32[32,512]{1,0:T(8,128)} %current.1) | copy-start | bytes 196612
  3.4 0.8 %copy-start.4 = (s32[32,512]{1,0:T(8,128)S(1)}, s32[32,512]{1,0:T(8,128)}, u32[]{:S(2)}) copy-start(s32[32,512]{1,0:T(8,128)} %mask.1) | copy-start | bytes 196612

commit v2 on v1

--- a/solution.py
+++ b/solution.py
@@ -84,7 +84,8 @@
 
 
 def step_kernel(
-    nr, nc, elevation, depth, friction, current, mask, out,
+    nr, nc, elevation_hbm, depth_hbm, friction_hbm, current_hbm, mask_hbm, out,
+    elevation, depth, friction, current, mask, in_sem,
     xbuf, kbuf, pbuf, x_send, x_recv, k_send, k_recv, p_send, p_recv,
 ):
     row_at, col_at = lax.axis_index("rows"), lax.axis_index("cols")
@@ -113,6 +114,18 @@
     for k in range(1, nc):
         pl.semaphore_signal(barrier, inc=1, device_id=col_peer(k), device_id_type=pl.DeviceIdType.MESH)
 
+    arrays = (
+        (depth_hbm, depth), (mask_hbm, mask), (friction_hbm, friction),
+        (elevation_hbm, elevation), (current_hbm, current),
+    )
+    loads = [
+        pltpu.make_async_copy(src, dst, in_sem.at[i]) for i, (src, dst) in enumerate(arrays)
+    ]
+    for load in loads:
+        load.start()
+
+    for load in loads[:3]:
+        load.wait()
     still = depth[...]
     wet = still * mask[...].astype(jnp.float32)
     damping = friction[...] / (4.0 * still)
@@ -120,26 +133,9 @@
     lane = lax.broadcasted_iota(jnp.int32, (height, width), 1)
     row = lax.broadcasted_iota(jnp.int32, (height, width), 0)
 
-    face = half_coupling * jnp.sqrt(wet * rolled(wet, -1, 0))
-    face = jnp.where(row == height - 1, 0.0, face)
-    unit_first = jnp.where(row == 0, 1.0, 0.0)
-    unit_last = jnp.where(row == height - 1, 1.0, 0.0)
-    from_first, from_last = reduce_lines(face, excess, [unit_first, unit_last], 0)
-    ends = (
-        from_first[0:1], from_first[height - 1 : height], from_last[height - 1 : height],
-        wet[0:1], wet[height - 1 : height],
-    )
-    for q, line in enumerate(ends):
-        for c in range(chunks):
-            kbuf[row_at, q, c : c + 1, :] = line[:, c * LANES : (c + 1) * LANES]
-
-    pl.semaphore_wait(barrier, nr + nc - 2)
-    k_copies = row_copies(kbuf, k_send, k_recv)
-    for copy in k_copies:
-        copy.start()
-
     face_x = half_coupling * jnp.sqrt(wet * rolled(wet, -1, 1))
     face_x = jnp.where(lane == width - 1, 0.0, face_x)
+    loads[3].wait()
     first_rhs = (1.0 - damping) * elevation[...]
     small = lax.broadcasted_iota(jnp.int32, (height, LANES), 1)
     at_left = col_at == 0
@@ -172,8 +168,26 @@
         )
         for k in range(1, nc)
     ]
+    pl.semaphore_wait(barrier, nr + nc - 2)
     for copy in x_copies:
         copy.start()
+
+    face = half_coupling * jnp.sqrt(wet * rolled(wet, -1, 0))
+    face = jnp.where(row == height - 1, 0.0, face)
+    unit_first = jnp.where(row == 0, 1.0, 0.0)
+    unit_last = jnp.where(row == height - 1, 1.0, 0.0)
+    from_first, from_last = reduce_lines(face, excess, [unit_first, unit_last], 0)
+    ends = (
+        from_first[0:1], from_first[height - 1 : height], from_last[height - 1 : height],
+        wet[0:1], wet[height - 1 : height],
+    )
+    for q, line in enumerate(ends):
+        for c in range(chunks):
+            kbuf[row_at, q, c : c + 1, :] = line[:, c * LANES : (c + 1) * LANES]
+    k_copies = row_copies(kbuf, k_send, k_recv)
+    for copy in k_copies:
+        copy.start()
+
     for copy in x_copies:
         copy.wait_recv()
 
@@ -208,6 +222,7 @@
             right_of = jnp.where(here, first[k + 1], right_of)
         half_step = solved + from_left * entering - from_right * leaving
 
+    loads[4].wait()
     courant = current[...]
     forward = jnp.where(lane == width - 1, right_of, rolled(half_step, -1, 1))
     backward = jnp.where(lane == 0, left_of, rolled(half_step, 1, 1))
@@ -263,9 +278,12 @@
     return pl.pallas_call(
         functools.partial(step_kernel, nr, nc),
         out_shape=jax.ShapeDtypeStruct(elevation.shape, jnp.float32),
-        in_specs=[pl.BlockSpec(memory_space=pltpu.VMEM)] * 5,
+        in_specs=[pl.BlockSpec(memory_space=pl.ANY)] * 5,
         out_specs=pl.BlockSpec(memory_space=pltpu.VMEM),
-        scratch_shapes=[
+        scratch_shapes=[pltpu.VMEM(elevation.shape, jnp.float32)] * 4
+        + [
+            pltpu.VMEM(elevation.shape, jnp.int32),
+            pltpu.SemaphoreType.DMA((5,)),
             pltpu.VMEM((nc, height, LANES), jnp.float32),
             pltpu.VMEM((nr, 5, chunks, LANES), jnp.float32),
             pltpu.VMEM((nr, 2, chunks, LANES), jnp.float32),
@@ -277,7 +295,7 @@
             pltpu.SemaphoreType.DMA((nr - 1,)),
         ],
         compiler_params=pltpu.CompilerParams(
-            collective_id=0, has_side_effects=True, vmem_limit_bytes=32 * 1024 * 1024
+            collective_id=0, has_side_effects=True, vmem_limit_bytes=60 * 1024 * 1024
         ),
     )(elevation, water_depth, friction, current_x, wet_mask)
 

time: 19.6 us -> 16.9 us (0.86)
  local copies, waits for them, and re-layouts: 4.83 us -> 1.47 us
  Pallas kernels: 14.4 us -> 15.3 us
    unnamed x11 -> x1, local copies, waits for them, and re-layouts: 4.83 us -> 1.47 us
    pallas_call x1, Pallas kernels: 14.4 us -> 15.3 us  [on_device(): pl.pallas_call(functools.partial(step_kernel, nr, nc), out_shape=jax.Shap...]
where the time goes in v2:
time: 16.9 us; the launch traced here: 16.7 us
  Pallas kernels  15.3 us (91%)
  local copies, waits for them, and re-layouts  1.47 us (9%)
    pallas_call x1, Pallas kernels, on_device(): pl.pallas_call(functools.partial(step_kernel, nr, nc), out_shape=jax.Shap...  15.3 us
    unnamed x1, local copies, waits for them, and re-layouts  1.47 us

profile of v2, /device:TPU:0, one launch (start us, length us, event | category | flops | bytes accessed | tf_op | source)
XLA Modules:
  0.0 16.7 jit_solution(605483101050166924)
XLA Ops:
  0.0 15.3 %shard_map.55 = f32[32,512]{1,0:T(8,128)} custom-call(f32[32,512]{1,0:T(8,128)} %elevation_hbm.1, f32[32,512]{1,0:T(8,128)} %depth_hbm.1, f32[32,512]{1,0:T(8,128)} %friction_hbm.1, f32[32,512]{1,0:T(8,128)} %current_hbm.1, s32[32,512]{1,0:T(8,128)} %mask_hbm.1), custom_call_target="tpu_custom_call" | custom-call | tf_op jit(solution)/shard_map/pallas_call | solution.py:278
  15.3 1.5 %copy.7 = f32[32,512]{1,0:T(8,128)} copy(f32[32,512]{1,0:T(8,128)} %shard_map.55) | data formatting | bytes 131072

commit v3 on v2

--- a/solution.py
+++ b/solution.py
@@ -19,27 +19,34 @@
     length = face.shape[axis]
     before = rolled(face, 1, axis)
     stride = 1
+    steps = []
+
+    def advance(right, to_next, to_prev, stride):
+        return (
+            right
+            + rolled(to_next * right, stride, axis)
+            + rolled(to_prev * right, -stride, axis)
+        )
+
     while stride < length:
         inverse = 1.0 / (excess + before + face)
         to_next = face * inverse
         to_prev = before * inverse
         through = to_next * before
-        excess = (
-            excess
-            + rolled(to_next * excess, stride, axis)
-            + rolled(to_prev * excess, -stride, axis)
-        )
-        rights = [
-            right
-            + rolled(to_next * right, stride, axis)
-            + rolled(to_prev * right, -stride, axis)
-            for right in rights
-        ]
+        excess = advance(excess, to_next, to_prev, stride)
+        rights = [advance(right, to_next, to_prev, stride) for right in rights]
+        steps.append((to_next, to_prev, stride))
         face = rolled(through, -stride, axis)
         before = rolled(through, stride, axis)
         stride *= 2
     inverse = 1.0 / excess
-    return [right * inverse for right in rights]
+
+    def solve(right):
+        for step in steps:
+            right = advance(right, *step)
+        return right * inverse
+
+    return [right * inverse for right in rights], solve
 
 
 def reduce_fluxes(lower, middle, upper, rights):
@@ -98,21 +105,18 @@
     def col_peer(offset):
         return (row_at, lax.rem(col_at + offset, nc))
 
-    def row_copies(buffer, send, recv):
-        return [
+    def send_rows(buffer, send, recv):
+        for k in range(nr - 1):
+            peer = jnp.where(k >= row_at, k + 1, k)
             pltpu.make_async_remote_copy(
                 src_ref=buffer.at[row_at], dst_ref=buffer.at[row_at],
-                send_sem=send.at[k - 1], recv_sem=recv.at[k - 1],
-                device_id=row_peer(k), device_id_type=pl.DeviceIdType.MESH,
-            )
-            for k in range(1, nr)
-        ]
-
-    barrier = pltpu.get_barrier_semaphore()
-    for k in range(1, nr):
-        pl.semaphore_signal(barrier, inc=1, device_id=row_peer(k), device_id_type=pl.DeviceIdType.MESH)
-    for k in range(1, nc):
-        pl.semaphore_signal(barrier, inc=1, device_id=col_peer(k), device_id_type=pl.DeviceIdType.MESH)
+                send_sem=send, recv_sem=recv,
+                device_id=(peer, col_at), device_id_type=pl.DeviceIdType.MESH,
+            ).start()
+
+    def wait_rows(buffer, semaphore):
+        part = buffer.at[pl.ds(0, nr - 1)]
+        pltpu.make_async_copy(part, part, semaphore).wait()
 
     arrays = (
         (depth_hbm, depth), (mask_hbm, mask), (friction_hbm, friction),
@@ -124,6 +128,12 @@
     for load in loads:
         load.start()
 
+    barrier = pltpu.get_barrier_semaphore()
+    for k in range(1, nr):
+        pl.semaphore_signal(barrier, inc=1, device_id=row_peer(k), device_id_type=pl.DeviceIdType.MESH)
+    for k in range(1, nc):
+        pl.semaphore_signal(barrier, inc=1, device_id=col_peer(k), device_id_type=pl.DeviceIdType.MESH)
+
     for load in loads[:3]:
         load.wait()
     still = depth[...]
@@ -142,15 +152,16 @@
     if nc == 2:
         edge = jnp.where(at_left, width - 1, 0)
         unit = jnp.where(lane == edge, 1.0, 0.0)
-        solved, spike = reduce_lines(face_x, excess, [first_rhs, unit], 1)
-        message = None
-        for q, values in enumerate((solved, spike, wet)):
+        (spike,), solve_x = reduce_lines(face_x, excess, [unit], 1)
+        message = jnp.sum(spike * first_rhs, axis=1, keepdims=True)
+        for q, values in ((1, spike), (2, wet)):
             chunk = jnp.where(at_left, values[:, width - LANES :], values[:, :LANES])
             chunk = pltpu.roll(chunk, q + jnp.where(at_left, 1, 0), 1)
-            message = chunk if q == 0 else jnp.where(small == q, chunk, message)
+            message = jnp.where(small == q, chunk, message)
     else:
         units = [jnp.where(lane == 0, 1.0, 0.0), jnp.where(lane == width - 1, 1.0, 0.0)]
-        solved, from_left, from_right = reduce_lines(face_x, excess, [first_rhs] + units, 1)
+        (from_left, from_right), solve_x = reduce_lines(face_x, excess, units, 1)
+        solved = solve_x(first_rhs)
         message = jnp.zeros((height, LANES), jnp.float32)
         columns = (
             solved[:, 0:1], solved[:, width - 1 : width], from_left[:, 0:1],
@@ -176,7 +187,7 @@
     face = jnp.where(row == height - 1, 0.0, face)
     unit_first = jnp.where(row == 0, 1.0, 0.0)
     unit_last = jnp.where(row == height - 1, 1.0, 0.0)
-    from_first, from_last = reduce_lines(face, excess, [unit_first, unit_last], 0)
+    (from_first, from_last), solve_y = reduce_lines(face, excess, [unit_first, unit_last], 0)
     ends = (
         from_first[0:1], from_first[height - 1 : height], from_last[height - 1 : height],
         wet[0:1], wet[height - 1 : height],
@@ -184,9 +195,9 @@
     for q, line in enumerate(ends):
         for c in range(chunks):
             kbuf[row_at, q, c : c + 1, :] = line[:, c * LANES : (c + 1) * LANES]
-    k_copies = row_copies(kbuf, k_send, k_recv)
-    for copy in k_copies:
-        copy.start()
+    send_rows(kbuf, k_send, k_recv)
+    if nc == 2:
+        solved = solve_x(first_rhs)
 
     for copy in x_copies:
         copy.wait_recv()
@@ -235,14 +246,11 @@
         line = jnp.sum(response * second_rhs, axis=0, keepdims=True)
         for c in range(chunks):
             pbuf[row_at, q, c : c + 1, :] = line[:, c * LANES : (c + 1) * LANES]
-    p_copies = row_copies(pbuf, p_send, p_recv)
-    for copy in p_copies:
-        copy.start()
-
-    (solved_y,) = reduce_lines(face, excess, [second_rhs], 0)
-
-    for copy in k_copies:
-        copy.wait_recv()
+    send_rows(pbuf, p_send, p_recv)
+
+    solved_y = solve_y(second_rhs)
+
+    wait_rows(kbuf, k_recv)
     ff, fl, ll, wf, wl = ([kbuf[k, q] for k in range(nr)] for q in range(5))
     weights = [half_coupling * jnp.sqrt(wl[k] * wf[k + 1]) for k in range(nr - 1)]
     system = flux_system(weights, ff, fl, ll)
@@ -252,8 +260,11 @@
     ]
     into, outof = reduce_fluxes(*system, rights)
 
-    for copy in p_copies:
-        copy.wait_recv()
+    for copy in x_copies:
+        copy.wait_send()
+    wait_rows(kbuf, k_send)
+    wait_rows(pbuf, p_send)
+    wait_rows(pbuf, p_recv)
     entering = leaving = jnp.zeros((chunks, LANES), jnp.float32)
     for k in range(nr - 1):
         jump = pbuf[k, 1] - pbuf[k + 1, 0]
@@ -266,9 +277,6 @@
             + from_first[:, at] * entering[c : c + 1, :]
             - from_last[:, at] * leaving[c : c + 1, :]
         )
-
-    for copy in k_copies + x_copies + p_copies:
-        copy.wait_send()
 
 
 def on_device(elevation, water_depth, friction, current_x, wet_mask):
@@ -289,13 +297,13 @@
             pltpu.VMEM((nr, 2, chunks, LANES), jnp.float32),
             pltpu.SemaphoreType.DMA((nc - 1,)),
             pltpu.SemaphoreType.DMA((nc - 1,)),
-            pltpu.SemaphoreType.DMA((nr - 1,)),
-            pltpu.SemaphoreType.DMA((nr - 1,)),
-            pltpu.SemaphoreType.DMA((nr - 1,)),
-            pltpu.SemaphoreType.DMA((nr - 1,)),
+            pltpu.SemaphoreType.DMA,
+            pltpu.SemaphoreType.DMA,
+            pltpu.SemaphoreType.DMA,
+            pltpu.SemaphoreType.DMA,
         ],
         compiler_params=pltpu.CompilerParams(
-            collective_id=0, has_side_effects=True, vmem_limit_bytes=60 * 1024 * 1024
+            collective_id=0, has_side_effects=True, vmem_limit_bytes=55150 * 1024
         ),
     )(elevation, water_depth, friction, current_x, wet_mask)
 

time: 16.9 us -> 15 us (0.89)
  Pallas kernels: 15.3 us -> 14.2 us
  local copies, waits for them, and re-layouts: 1.47 us -> 0.63 us
    pallas_call x1, Pallas kernels: 15.3 us -> 14.2 us  [on_device(): pl.pallas_call(functools.partial(step_kernel, nr, nc), out_shape=jax.Shap...]
    unnamed x1, local copies, waits for them, and re-layouts: 1.47 us -> 0.63 us
where the time goes in v3:
time: 15 us; the launch traced here: 14.9 us
  Pallas kernels  14.2 us (95%)
  local copies, waits for them, and re-layouts  0.63 us (4%)
    pallas_call x1, Pallas kernels, on_device(): pl.pallas_call(functools.partial(step_kernel, nr, nc), out_shape=jax.Shap...  14.2 us
    unnamed x1, local copies, waits for them, and re-layouts  0.63 us

profile of v3, /device:TPU:0, one launch (start us, length us, event | category | flops | bytes accessed | tf_op | source)
XLA Modules:
  0.0 14.9 jit_solution(8214397321367003186)
XLA Ops:
  0.0 14.2 %shard_map.55 = f32[32,512]{1,0:T(8,128)S(1)} custom-call(f32[32,512]{1,0:T(8,128)} %elevation_hbm.1, f32[32,512]{1,0:T(8,128)} %depth_hbm.1, f32[32,512]{1,0:T(8,128)} %friction_hbm.1, f32[32,512]{1,0:T(8,128)} %current_hbm.1, s32[32,512]{1,0:T(8,128)} %mask_hbm.1), custom_call_target="tpu_custom_call" | custom-call | tf_op jit(solution)/shard_map/pallas_call | solution.py:286
  14.2 0.6 %copy.7 = f32[32,512]{1,0:T(8,128)} copy(f32[32,512]{1,0:T(8,128)S(1)} %shard_map.55) | data formatting | bytes 131072

commit v4 on v3

--- a/solution.py
+++ b/solution.py
@@ -152,12 +152,12 @@
     if nc == 2:
         edge = jnp.where(at_left, width - 1, 0)
         unit = jnp.where(lane == edge, 1.0, 0.0)
-        (spike,), solve_x = reduce_lines(face_x, excess, [unit], 1)
-        message = jnp.sum(spike * first_rhs, axis=1, keepdims=True)
-        for q, values in ((1, spike), (2, wet)):
+        (spike, solved), _ = reduce_lines(face_x, excess, [unit, first_rhs], 1)
+        message = None
+        for q, values in enumerate((solved, spike, wet)):
             chunk = jnp.where(at_left, values[:, width - LANES :], values[:, :LANES])
             chunk = pltpu.roll(chunk, q + jnp.where(at_left, 1, 0), 1)
-            message = jnp.where(small == q, chunk, message)
+            message = chunk if q == 0 else jnp.where(small == q, chunk, message)
     else:
         units = [jnp.where(lane == 0, 1.0, 0.0), jnp.where(lane == width - 1, 1.0, 0.0)]
         (from_left, from_right), solve_x = reduce_lines(face_x, excess, units, 1)
@@ -196,9 +196,6 @@
         for c in range(chunks):
             kbuf[row_at, q, c : c + 1, :] = line[:, c * LANES : (c + 1) * LANES]
     send_rows(kbuf, k_send, k_recv)
-    if nc == 2:
-        solved = solve_x(first_rhs)
-
     for copy in x_copies:
         copy.wait_recv()
 

time: 15 us -> 14.8 us (0.987)
  Pallas kernels: 14.2 us -> 14 us
    pallas_call x1, Pallas kernels: 14.2 us -> 14 us  [on_device(): pl.pallas_call(functools.partial(step_kernel, nr, nc), out_shape=jax.Shap...]
where the time goes in v4:
time: 14.8 us; the launch traced here: 14.6 us
  Pallas kernels  14 us (95%)
  local copies, waits for them, and re-layouts  0.63 us (4%)
    pallas_call x1, Pallas kernels, on_device(): pl.pallas_call(functools.partial(step_kernel, nr, nc), out_shape=jax.Shap...  14 us
    unnamed x1, local copies, waits for them, and re-layouts  0.63 us

profile of v4, /device:TPU:0, one launch (start us, length us, event | category | flops | bytes accessed | tf_op | source)
XLA Modules:
  0.0 14.6 jit_solution(11842961096439018806)
XLA Ops:
  0.0 14.0 %shard_map.55 = f32[32,512]{1,0:T(8,128)S(1)} custom-call(f32[32,512]{1,0:T(8,128)} %elevation_hbm.1, f32[32,512]{1,0:T(8,128)} %depth_hbm.1, f32[32,512]{1,0:T(8,128)} %friction_hbm.1, f32[32,512]{1,0:T(8,128)} %current_hbm.1, s32[32,512]{1,0:T(8,128)} %mask_hbm.1), custom_call_target="tpu_custom_call" | custom-call | tf_op jit(solution)/shard_map/pallas_call | solution.py:283
  14.0 0.6 %copy.7 = f32[32,512]{1,0:T(8,128)} copy(f32[32,512]{1,0:T(8,128)S(1)} %shard_map.55) | data formatting | bytes 131072

commit v5 on v4

--- a/solution.py
+++ b/solution.py
@@ -196,6 +196,12 @@
         for c in range(chunks):
             kbuf[row_at, q, c : c + 1, :] = line[:, c * LANES : (c + 1) * LANES]
     send_rows(kbuf, k_send, k_recv)
+    loads[4].wait()
+    half_courant = 0.5 * current[...]
+    half_square = half_courant * current[...]
+    ahead, behind = half_square - half_courant, half_square + half_courant
+    centre = (1.0 - damping) - 2.0 * half_square
+
     for copy in x_copies:
         copy.wait_recv()
 
@@ -230,14 +236,9 @@
             right_of = jnp.where(here, first[k + 1], right_of)
         half_step = solved + from_left * entering - from_right * leaving
 
-    loads[4].wait()
-    courant = current[...]
     forward = jnp.where(lane == width - 1, right_of, rolled(half_step, -1, 1))
     backward = jnp.where(lane == 0, left_of, rolled(half_step, 1, 1))
-    advected = 0.5 * courant * (forward - backward) - 0.5 * courant * courant * (
-        forward - 2.0 * half_step + backward
-    )
-    second_rhs = (1.0 - damping) * half_step - advected
+    second_rhs = centre * half_step + ahead * forward + behind * backward
 
     for q, response in enumerate((from_first, from_last)):
         line = jnp.sum(response * second_rhs, axis=0, keepdims=True)

time: 14.8 us -> 14.7 us (level)
  no operation moved by 1% of the time
where the time goes in v5:
time: 14.7 us; the launch traced here: 14.5 us
  Pallas kernels  13.9 us (95%)
  local copies, waits for them, and re-layouts  0.63 us (4%)
    pallas_call x1, Pallas kernels, on_device(): pl.pallas_call(functools.partial(step_kernel, nr, nc), out_shape=jax.Shap...  13.9 us
    unnamed x1, local copies, waits for them, and re-layouts  0.63 us

profile of v5, /device:TPU:0, one launch (start us, length us, event | category | flops | bytes accessed | tf_op | source)
XLA Modules:
  0.0 14.5 jit_solution(7244653495606786527)
XLA Ops:
  0.0 13.9 %shard_map.55 = f32[32,512]{1,0:T(8,128)S(1)} custom-call(f32[32,512]{1,0:T(8,128)} %elevation_hbm.1, f32[32,512]{1,0:T(8,128)} %depth_hbm.1, f32[32,512]{1,0:T(8,128)} %friction_hbm.1, f32[32,512]{1,0:T(8,128)} %current_hbm.1, s32[32,512]{1,0:T(8,128)} %mask_hbm.1), custom_call_target="tpu_custom_call" | custom-call | tf_op jit(solution)/shard_map/pallas_call | solution.py:284
  13.9 0.6 %copy.7 = f32[32,512]{1,0:T(8,128)} copy(f32[32,512]{1,0:T(8,128)S(1)} %shard_map.55) | data formatting | bytes 131072
